TPU v7x, 32 devices: a whole 2x2x4 slice. The times are simulated.
32 devices in a mesh: segment: 4 (over y, x), dp: 8 (over z, core).
Axes of the slice: x: 2, y: 2, z: 4, core: 2. Of those that a mesh axis runs over, the one named last changes fastest.
Arguments:
- inputs: bfloat16 [8, 8, 576, 128], P('segment', 'dp'), may hold values from -6 to 6
- grid_size: int32 [8, 8, 2], P(None, 'dp'), may hold values from 12 to 24, as said below
- keep_mask: int32 [8, 8, 4], P(None, 'dp'), may hold values 0 or 1
- cotangent: bfloat16 [8, 8, 576, 128], P('segment', 'dp'), may hold values from -6 to 6
- norm_gain: float32 [2, 4, 128], replicated, may hold values from 0.5 to 1.5
- norm_shift: float32 [2, 4, 128], replicated, may hold values from -1.5 to 1.5
- query_weight: bfloat16 [2, 128, 128], replicated, may hold values from -0.5 to 0.5
- query_bias: float32 [2, 128], replicated, may hold values from -1.5 to 1.5
- pool_four: bfloat16 [2, 2048, 128], replicated, may hold values from -0.125 to 0.125
- pool_two: bfloat16 [2, 512, 128], replicated, may hold values from -0.25 to 0.25
- keyval_weight: bfloat16 [2, 2, 128, 128], replicated, may hold values from -0.5 to 0.5
- value_bias: float32 [2, 2, 64], replicated, may hold values from -1.5 to 1.5
- local_kernel: float32 [2, 2, 9, 64], replicated, may hold values from -1 to 1
- proj_weight: bfloat16 [2, 128, 128], replicated, may hold values from -1.5 to 1.5
- proj_bias: float32 [2, 128], replicated, may hold values from -1.5 to 1.5
- hidden_weight: bfloat16 [2, 128, 1024], replicated, may hold values from -0.5 to 0.5
- hidden_bias: float32 [2, 1024], replicated, may hold values from -1.5 to 1.5
- mixer_kernel: float32 [2, 9, 1024], replicated, may hold values from -1 to 1
- mixer_bias: float32 [2, 1024], replicated, may hold values from -1.5 to 1.5
- output_weight: bfloat16 [2, 1024, 128], replicated, may hold values from -0.1875 to 0.1875
- output_bias: float32 [2, 128], replicated, may hold values from -1.5 to 1.5
Outputs:
- outputs: bfloat16 [8, 8, 576, 128], P('segment', 'dp')
- input_grad: bfloat16 [8, 8, 576, 128], P('segment', 'dp')
- grad_norm_gain: float32 [2, 4, 128], replicated
- grad_norm_shift: float32 [2, 4, 128], replicated
- grad_query_weight: float32 [2, 128, 128], replicated
- grad_query_bias: float32 [2, 128], replicated
- grad_pool_four: float32 [2, 2048, 128], replicated
- grad_pool_two: float32 [2, 512, 128], replicated
- grad_keyval_weight: float32 [2, 2, 128, 128], replicated
- grad_value_bias: float32 [2, 2, 64], replicated
- grad_local_kernel: float32 [2, 2, 9, 64], replicated
- grad_proj_weight: float32 [2, 128, 128], replicated
- grad_proj_bias: float32 [2, 128], replicated
- grad_hidden_weight: float32 [2, 128, 1024], replicated
- grad_hidden_bias: float32 [2, 1024], replicated
- grad_mixer_kernel: float32 [2, 9, 1024], replicated
- grad_mixer_bias: float32 [2, 1024], replicated
- grad_output_weight: float32 [2, 1024, 128], replicated
- grad_output_bias: float32 [2, 128], replicated
Inputs may be any that keep to these rules, and one draw needn't show every extreme that they name: `grid_size`: rows then columns of valid patches, top-left aligned; for every image one of the two equals 24.
All inputs are finite; a program needn't handle non-finite values. No bound on the sum of `keep_mask` on one device may be relied on, other than what follows from the above.
Results may differ from a plain program's by a relative error of at most 0.019.
Values may be sent and summed in bfloat16 or wider, within the bound.
A program may use at most 256 MiB of HBM per device.

v0:
```python
import functools

import jax
import jax.numpy as jnp
import numpy as np
from jax import lax
from jax.experimental import pallas as pl
from jax.experimental.pallas import tpu as pltpu
from jax.sharding import PartitionSpec as P

GRID = 24
TOK = GRID * GRID
C = 128
FF = 1024
HEAD = 32
BLOCKS = 2
SIDES = (6, 12)
STRIDES = (4, 2)
CELLS = (48, 144)
SEGS = ((0, 48), (48, 96), (96, 240), (240, 384))
KEYS = 384
PERM = 16 * 48 + 4 * 144
TAPS = 9
UW = TAPS * C + C
CHUNK = 512
TILE = 96

R_P4, R_P2, R_KV, R_Q, R_PROJ, R_ATT = 0, 2048, 2560, 2816, 2944, 3072
R_MLP = 2048
ATT_AT = (R_ATT, 0)
MLP_AT = (2 * R_ATT + R_MLP, 2 * R_ATT)
S_GAIN, S_SHIFT, S_QB, S_VB, S_PB, S_OB, S_LK, S_HB, S_MB, S_MK, S_BLOCK = (
    0,
    4,
    8,
    9,
    10,
    11,
    16,
    32,
    40,
    48,
    192,
)
R_SMALL = BLOCKS * (R_ATT + R_MLP)
ROWS = R_SMALL + 512
PIECES = (
    (ATT_AT[1], R_ATT),
    (ATT_AT[0], R_ATT),
    (MLP_AT[1], R_MLP),
    (MLP_AT[0], R_MLP // 2),
    (MLP_AT[0] + R_MLP // 2, R_MLP // 2 + ROWS - R_SMALL),
)

QW, P4, P2, KVW, LK, PW, HW, MK, OW = 2, 4, 5, 6, 8, 9, 11, 13, 15

epsilon = 1e-06
keep_rate = 0.8
ROOT = HEAD**-0.5
LOG2E = 1.4426950408889634
f32, bf16 = jnp.float32, jnp.bfloat16


def hidden_row(tile):
    return tile // (CHUNK // C) * 2 * CHUNK + tile % (CHUNK // C) * C


def output_row(step):
    return step * 2 * CHUNK + CHUNK


def patch_tokens():
    tokens = np.full((8, PERM), -1.0, np.float32)
    base = 0
    for stride, side, cells in zip(STRIDES, SIDES, CELLS):
        for row_off in range(stride):
            for col_off in range(stride):
                for a in range(side):
                    for b in range(side):
                        token = (a * stride + row_off) * GRID + b * stride + col_off
                        tokens[:, base + a * side + b] = token
                base += cells
    return tokens


def cell_places():
    places = np.full((2, sum(CELLS), 128), 99.0, np.float32)
    base = 0
    for side, cells in zip(SIDES, CELLS):
        for a in range(side):
            for b in range(side):
                places[0, base + a * side + b] = a
                places[1, base + a * side + b] = b
        base += cells
    return places


def nn(left, right):
    return jnp.dot(left, right, preferred_element_type=f32)


def nt(left, right):
    return lax.dot_general(left, right, (((1,), (1,)), ((), ())), preferred_element_type=f32)


def tn(left, right):
    return lax.dot_general(left, right, (((0,), (0,)), ((), ())), preferred_element_type=f32)


def gelu_parts(m):
    size = jnp.abs(m)
    t = pl.reciprocal(1.0 + (0.3275911 * 0.5**0.5) * size, approx=True)
    e = jnp.exp2(m * (m * (-0.5 * LOG2E)))
    poly = 0.5 * 1.061405429
    for coef in (-1.453152027, 1.421413741, -0.284496736, 0.254829592):
        poly = poly * t + 0.5 * coef
    poly = poly * t
    tail = poly * e
    slope = (poly - size * 0.3989422804014327) * e
    return jnp.maximum(m, 0.0) - size * tail, jnp.where(m >= 0, 1.0 - slope, slope)


def norm_parts(x):
    centred = x - jnp.mean(x, axis=-1, keepdims=True)
    scale = lax.rsqrt(jnp.mean(centred * centred, axis=-1, keepdims=True) + epsilon)
    return centred * scale, scale


def norm_back(du, xhat, scale, gain):
    dxhat = du * gain
    first = jnp.mean(dxhat, axis=-1, keepdims=True)
    second = jnp.mean(dxhat * xhat, axis=-1, keepdims=True)
    return scale * (dxhat - first - xhat * second)


def col_sum(x):
    return jnp.sum(x, axis=0, keepdims=True)


def folded(x):
    return jnp.sum(x.reshape(-1, 8, x.shape[-1]), axis=0)


class Summed:
    STEPS = 7

    def __init__(self, place, piece, base, count, refs):
        self.seg, self.dp, self.segments, self.inner, self.outer = place
        self.piece, self.base = piece, base
        (
            self.src,
            self.half_in,
            self.quarter_in,
            self.part_in,
            self.whole_in,
            self.own,
            self.total,
            self.send,
            self.recv,
        ) = refs
        self.core, rest = self.dp % 2, self.dp // 2
        self.part, self.group = rest % self.inner, rest // self.inner
        self.half = count // 2
        self.quarter = self.half // self.segments
        self.share = self.quarter // self.inner
        quarters, shares = (self.segments - 1) * self.quarter, (self.inner - 1) * self.share
        self.moved = (self.half, quarters, shares, shares, quarters, self.half)
        self.at_quarter = self.seg * self.quarter
        self.at_share = self.at_quarter + self.part * self.share

    def span(self, start, size):
        return pl.ds(pl.multiple_of(start, 16), size)

    def device(self, seg=None, core=None, part=None, group=None):
        seg = self.seg if seg is None else seg
        core = self.core if core is None else core
        part = self.part if part is None else part
        group = self.group if group is None else group
        return (seg, (group * self.inner + part) * 2 + core)

    def copy(self, k, src, dst, device):
        return pltpu.make_async_remote_copy(
            src_ref=src,
            dst_ref=dst,
            send_sem=self.send.at[self.piece],
            recv_sem=self.recv.at[self.piece, k],
            device_id=device,
            device_id_type=pl.DeviceIdType.MESH,
        )

    def counted(self, k, count):
        ref = self.total.at[pl.ds(0, count), :]
        return self.copy(k, ref, ref, self.device(core=1 - self.core))

    def step(self, k):
        if k > 0:
            self.counted(k - 1, self.moved[k - 1]).wait_recv()
            self.gather(k)
        if k + 1 < self.STEPS:
            self.depart(k)

    def drain(self):
        count = sum(self.moved) + (self.outer - 1) * self.share
        self.counted(0, count).wait_send()

    def depart(self, k):
        half = self.base // 2
        mine = self.base + self.core * self.half
        if k == 0:
            src = self.src.at[self.span(self.base + (1 - self.core) * self.half, self.half), :]
            dst = self.half_in.at[self.span(half, self.half), :]
            self.copy(k, src, dst, self.device(core=1 - self.core)).start()
        elif k == 1:
            at = self.span(half // self.segments, self.quarter)
            for d in range(1, self.segments):
                to = self.seg ^ d
                src = self.own.at[self.span(half + to * self.quarter, self.quarter), :]
                dst = self.quarter_in.at[d - 1, at, :]
                self.copy(k, src, dst, self.device(seg=to)).start()
        elif k == 2:
            at = self.span(self.share_in(), self.share)
            for d in range(1, self.inner):
                to = self.part ^ d
                start = half + self.at_quarter + to * self.share
                src = self.own.at[self.span(start, self.share), :]
                self.copy(k, src, self.part_in.at[d - 1, at, :], self.device(part=to)).start()
        elif k == 3:
            ref = self.total.at[self.span(mine + self.at_share, self.share), :]
            for d in range(1, self.inner):
                self.copy(k, ref, ref, self.device(part=self.part ^ d)).start()
        elif k == 4:
            ref = self.total.at[self.span(mine + self.at_quarter, self.quarter), :]
            for d in range(1, self.segments):
                self.copy(k, ref, ref, self.device(seg=self.seg ^ d)).start()
        else:
            ref = self.total.at[self.span(mine, self.half), :]
            self.copy(k, ref, ref, self.device(core=1 - self.core)).start()

    def share_in(self):
        return self.base // 2 // self.segments // self.inner

    def gather(self, k):
        half = self.base // 2
        if k == 1:
            first = (self.src, self.base + self.core * self.half)
            self.add((self.own, half), first, [(self.half_in, half)], self.half)
        elif k == 2:
            mine = (self.own, half + self.at_quarter)
            at = half // self.segments
            received = [(self.quarter_in.at[d], at) for d in range(self.segments - 1)]
            self.add(mine, mine, received, self.quarter)
        elif k == 3:
            received = [(self.part_in.at[d], self.share_in()) for d in range(self.inner - 1)]
            mine = (self.own, half + self.at_share)
            into = (self.total, self.base + self.core * self.half + self.at_share)
            if self.outer > 1:
                self.add(mine, mine, received, self.share)
                slot = self.STEPS - 1
                src = self.own.at[self.span(mine[1], self.share), :]
                at = self.span(self.share_in(), self.share)
                for d in range(1, self.outer):
                    to = self.device(group=self.group ^ d)
                    self.copy(slot, src, self.whole_in.at[d - 1, at, :], to).start()
                self.counted(slot, (self.outer - 1) * self.share).wait_recv()
                received = [(self.whole_in.at[d], self.share_in()) for d in range(self.outer - 1)]
            self.add(into, mine, received, self.share)

    def add(self, dst, first, others, count):
        step = next(size for size in (128, 96, 80, 64, 48, 32, 16) if count % size == 0)

        def body(t, carry):
            at = t * step
            total = first[0][self.span(first[1] + at, step), :].astype(f32)
            for ref, start in others:
                total = total + ref[self.span(start + at, step), :].astype(f32)
            dst[0][self.span(dst[1] + at, step), :] = total.astype(bf16)
            return carry

        lax.fori_loop(0, count // step, body, 0)


def greet(seg, dp, segments, inner, outer):
    barrier = pltpu.get_barrier_semaphore()
    core, part, group = dp % 2, dp // 2 % inner, dp // 2 // inner
    peers = [(seg, dp + 1 - 2 * core)]
    peers += [(seg ^ d, dp) for d in range(1, segments)]
    peers += [(seg, (group * inner + (part ^ d)) * 2 + core) for d in range(1, inner)]
    peers += [(seg, ((group ^ d) * inner + part) * 2 + core) for d in range(1, outer)]
    for peer in peers:
        pl.semaphore_signal(
            barrier, inc=1, device_id=peer, device_id_type=pl.DeviceIdType.MESH
        )
    return lambda: pl.semaphore_wait(barrier, len(peers))


def sum_scratch(sizes):
    segments, inner, outer = sizes
    quarter = ROWS // 2 // segments
    share = quarter // inner
    return [
        pltpu.VMEM((ROWS // 2, C), bf16),
        pltpu.VMEM((segments - 1, quarter, C), bf16),
        pltpu.VMEM((inner - 1, share, C), bf16),
        pltpu.VMEM((max(outer - 1, 1), share, C), bf16),
        pltpu.VMEM((ROWS // 2, C), bf16),
        pltpu.VMEM((ROWS, C), bf16),
        pltpu.SemaphoreType.DMA((len(PIECES),)),
        pltpu.SemaphoreType.DMA((len(PIECES), Summed.STEPS)),
    ]


def compute_kernel(
    own,
    images,
    sizes,
    grid_ref,
    keep_ref,
    x_ref,
    cot_in,
    ng,
    ns,
    qw,
    qb,
    p4w,
    p2w,
    kvw,
    vb,
    lk,
    pw,
    pb,
    hw,
    hb,
    mk,
    mb,
    ow,
    ob,
    tokens,
    places,
    out_ref,
    dx_ref,
    summed_ref,
    xs,
    valid,
    um,
    u_all,
    ut,
    wc,
    ex,
    xh_a,
    xh_m,
    sc,
    u_a,
    q_a,
    p4,
    p2,
    xh_p,
    sc_p,
    ge_p,
    kin,
    wv,
    kb,
    vbd,
    pt,
    o_t,
    o_n,
    a_all,
    g_all,
    db,
    db_t,
    acc,
    kmask,
    near,
    small,
    pc,
    scale_ref,
    cot_ref,
    perm,
    perm_t,
    out_st,
    dx_st,
    sems,
    gp,
    half_in,
    quarter_in,
    part_in,
    whole_in,
    own_part,
    total_ref,
    send,
    recv,
):
    n = images
    rows = n * TOK
    seg, dp = lax.axis_index("segment"), lax.axis_index("dp")
    all_here = greet(seg, dp, *sizes)
    late = pltpu.make_async_copy(cot_in, cot_ref, sems.at[0])
    late.start()
    leaving = []

    def leave(src, dst):
        made = pltpu.make_async_copy(src, dst, sems.at[1 + len(leaving)])
        made.start()
        leaving.append(made)

    refs = (
        gp,
        half_in,
        quarter_in,
        part_in,
        whole_in,
        own_part,
        total_ref,
        send,
        recv,
    )
    pieces = [
        Summed((seg, dp) + sizes, p, base, count, refs) for p, (base, count) in enumerate(PIECES)
    ]

    def move(*steps):
        for p, k in steps:
            pieces[p].step(k)
            if k + 1 == Summed.STEPS:
                rows_of = pl.ds(PIECES[p][0], PIECES[p][1])
                leave(total_ref.at[rows_of, :], summed_ref.at[rows_of, :])

    def move_if(now, *steps):
        pl.when(now)(lambda: move(*steps))

    lane = lax.broadcasted_iota(jnp.int32, (8, 128), 1)[0:1]

    def head_lanes(h):
        return (lane >= h * HEAD) & (lane < (h + 1) * HEAD)

    def tiles(fn, step=TILE):
        sums = None
        for start in range(0, rows, step):
            got = fn(slice(start, start + step))
            if got is not None:
                sums = got if sums is None else [x + y for x, y in zip(sums, got)]
        return None if sums is None else [col_sum(x) for x in sums]

    def row(ref, j, k=None):
        return ref[j, pl.ds(k, 1), :] if k is not None else ref[pl.ds(j, 1), :]

    def put(at, value):
        small[pl.ds(at, 1), :] = value

    def packed(start, count):
        return pl.ds(pl.multiple_of(start, 128), count)

    def shifted_rows(v, by):
        if by == 0:
            return v
        pad = jnp.zeros((abs(by), v.shape[1]), v.dtype)
        if by > 0:
            return jnp.concatenate([v[by:], pad], axis=0)
        return jnp.concatenate([pad, v[:by]], axis=0)

    col = lax.broadcasted_iota(jnp.int32, (GRID, GRID, 128), 1).reshape(TOK, 128)

    def taps_of(v):
        left = jnp.where(col > 0, pltpu.roll(v, 1, 0), 0.0)
        right = jnp.where(col < GRID - 1, pltpu.roll(v, TOK - 1, 0), 0.0)
        for row_off in range(3):
            for col_off, piece in enumerate((left, v, right)):
                yield row_off * 3 + col_off, shifted_rows(piece, (row_off - 1) * GRID)

    small[...] = jnp.zeros_like(small)
    sizes = []
    lane_row = lax.broadcasted_iota(jnp.int32, (TOK, 128), 1)
    tap = lane % 32
    down, across_by = tap // 3 - 1, tap % 3 - 1
    tap_lane = (tap < TAPS) & (lane < 64)
    for i in range(n):
        m_id, d_id = seg * own + i // (n // own), i % (n // own)
        high, wide = grid_ref[d_id, 0, m_id], grid_ref[d_id, 1, m_id]
        sizes.append((high, wide))
        line = lax.broadcasted_iota(jnp.int32, (GRID, GRID, 128), 0).reshape(TOK, 128)
        good = jnp.where((line < high) & (col < wide), 1.0, 0.0)
        valid[i * TOK : (i + 1) * TOK, :] = good
        for k in range(2 * BLOCKS):
            kept = keep_ref[d_id, k, m_id].astype(f32) / keep_rate
            scale_ref[i, k] = kept
        near_row, near_col = line + down, col + across_by
        there = (near_row >= 0) & (near_row < high) & (near_col >= 0) & (near_col < wide)
        ones = (lane_row == 16) | (lane_row == 48)
        flags = jnp.where(ones | (there & tap_lane), 1.0, 0.0)
        for j in range(BLOCKS):
            u_all[j, i * TOK : (i + 1) * TOK, TAPS * C :] = flags.astype(bf16)
        base = 0
        for t in range(2):
            span = slice(base, base + CELLS[t])
            tall = (high + STRIDES[t] - 1) // STRIDES[t]
            across = (wide + STRIDES[t] - 1) // STRIDES[t]
            inside = (places[0, span, :] < tall.astype(f32)) & (
                places[1, span, :] < across.astype(f32)
            )
            kmask[i, span, :] = jnp.where(inside, 1.0, 0.0)
            base += CELLS[t]
    base = 0
    for t in range(2):
        span = slice(base, base + CELLS[t])
        a, b = places[0, span, :], places[1, span, :]
        for off in range(9):
            dr, dc = float(off // 3 - 1), float(off % 3 - 1)
            top = float(SIDES[t])
            ok = (a + dr >= 0) & (a + dr < top) & (b + dc >= 0) & (b + dc < top)
            near[off, span, :] = jnp.where(ok, 1.0, 0.0)
        base += CELLS[t]

    base = start = 0
    for t in range(2):
        span, stride = slice(start, start + CELLS[t]), STRIDES[t]
        corner = places[0, span, :] * float(stride * GRID) + places[1, span, :] * float(stride)
        for k in range(stride * stride):
            token = corner + float(k // stride * GRID + k % stride)
            for c0 in range(0, TOK, 128):
                width = min(128, TOK - c0)
                here = lax.broadcasted_iota(jnp.int32, (CELLS[t], width), 1).astype(f32) + float(c0)
                block = jnp.where(token[:, :width] == here, 1.0, 0.0)
                perm[base : base + CELLS[t], c0 : c0 + width] = block.astype(bf16)
            base += CELLS[t]
        start += CELLS[t]
    for r0 in range(0, TOK, TILE):
        here = lax.broadcasted_iota(jnp.int32, (TILE, PERM), 0).astype(f32) + float(r0)
        block = jnp.where(tokens[0:1, :] == here, 1.0, 0.0)
        perm_t[r0 : r0 + TILE, :] = block.astype(bf16)

    xs[...] = x_ref[...].astype(f32)

    def scaled(span, k):
        return valid[span, :] * scale_ref[span.start // TOK, k]

    def cell_spans(t):
        start = 0 if t == 0 else n * CELLS[0]
        return [slice(start + i * CELLS[t], start + (i + 1) * CELLS[t]) for i in range(n)]

    def cells_all(t):
        return slice(0, n * CELLS[0]) if t == 0 else slice(n * CELLS[0], n * sum(CELLS))

    place_span = (slice(0, CELLS[0]), slice(CELLS[0], sum(CELLS)))
    half = lane < 64
    own_half = (half, jnp.logical_not(half))

    def near_shift(t, off):
        return ((off // 3 - 1) * SIDES[t] + off % 3 - 1) % CELLS[t]

    def attention_forward(j):
        build_wc(j)

        def first(ts):
            xhat, scale = norm_parts(xs[ts, :])
            xh_a[j, ts, :] = xhat
            sc[j, ts, 0:1] = scale
            u_a[j, ts, :] = (xhat * row(ng, j, 0) + row(ns, j, 0)).astype(bf16)

        tiles(first)
        for i in range(n):
            span = slice(i * TOK, (i + 1) * TOK)
            u = u_a[j, span, :]
            q_a[j, span, :] = (nn(u, qw[j]) + row(qb, j)).astype(bf16)
            um[:, i * C : (i + 1) * C] = (u.astype(f32) * valid[span, :]).astype(bf16)
        pc[...] = nn(perm[...], um[...]).astype(bf16)
        base = 0
        for t, ref in enumerate((p4, p2)):
            for k in range(STRIDES[t] ** 2):
                for i in range(n):
                    ref[j, i * CELLS[t] : (i + 1) * CELLS[t], k * C : (k + 1) * C] = pc[
                        base : base + CELLS[t], i * C : (i + 1) * C
                    ]
                base += CELLS[t]
        for t, (ref, weight) in enumerate(((p4, p4w), (p2, p2w))):
            xhat, scale = norm_parts(nn(ref[j], weight[j]))
            act, slope = gelu_parts(xhat * row(ng, j, 1 + t) + row(ns, j, 1 + t))
            act = act.astype(bf16)
            span = cells_all(t)
            xh_p[j, span, :] = xhat
            sc_p[j, span, :] = jnp.broadcast_to(scale, xhat.shape)
            ge_p[j, span, :] = slope
            kin[j, span, :] = act
            keyval = nn(act, kvw[j, t])
            turned = pltpu.roll(keyval, 64, 1)
            keys, vals = (keyval, turned) if t == 0 else (turned, keyval)
            bias = jnp.concatenate([row(vb, j, 0), row(vb, j, 1)], axis=1)
            kernel = jnp.concatenate([lk[j, :, 0, :], lk[j, :, 1, :]], axis=1)
            for i in range(n):
                part = slice(i * CELLS[t], (i + 1) * CELLS[t])
                w = (vals[part] + bias) * kmask[i, place_span[t], :]
                wv[j, cell_spans(t)[i], :] = w
                v = w
                for off in range(9):
                    by = near_shift(t, off)
                    moved = pltpu.roll(w, (CELLS[t] - by) % CELLS[t], 0) if by else w
                    v = v + moved * (near[off, place_span[t], :] * kernel[off : off + 1])
                for h in (2 * t, 2 * t + 1):
                    seg_rows = slice(*SEGS[h])
                    kb[j, i, seg_rows, :] = jnp.where(head_lanes(h), keys[part], 0.0).astype(bf16)
                    vbd[j, i, seg_rows, :] = jnp.where(head_lanes(h), v, 0.0).astype(bf16)
        for i in range(n):
            span = slice(i * TOK, (i + 1) * TOK)
            scores = nt(kb[j, i], q_a[j, span, :])
            for h, (low, top) in enumerate(SEGS):
                mask = kmask[i, place_span[h // 2], 0:1] > 0
                for c0 in range(0, TOK, 128):
                    c1 = min(c0 + 128, TOK)
                    s = jnp.where(mask, scores[low:top, c0:c1], -1e30)
                    e = jnp.exp2((s - jnp.max(s, axis=0, keepdims=True)) * (ROOT * LOG2E))
                    weight = e * pl.reciprocal(jnp.sum(e, axis=0, keepdims=True), approx=True)
                    pt[j, i, low:top, c0:c1] = weight.astype(bf16)
            mixed = tn(vbd[j, i], pt[j, i])
            o_t[j, i] = mixed.astype(bf16)
            o_n[span, :] = mixed.T.astype(bf16)
        for i in range(n):
            span = slice(i * TOK, (i + 1) * TOK)
            branch = nn(o_n[span, :], pw[j]) + row(pb, j)
            xs[span, :] = (xs[span, :] + scaled(span, 2 * j) * branch).astype(bf16).astype(f32)

    def build_wc(j):
        bias = row(hb, j)
        for r0 in range(0, C, 16):
            weight = hw[j, r0 : r0 + 16, :].astype(f32)
            for off in range(TAPS):
                factor = mk[off, pl.ds(j, 1), :] + (1.0 if off == 4 else 0.0)
                wc[j, off * C + r0 : off * C + r0 + 16, :] = (weight * factor).astype(bf16)
        ex[...] = jnp.zeros_like(ex)
        for off in range(TAPS + 1):
            at = off if off < TAPS else 16
            value = bias * mk[off, pl.ds(j, 1), :] if off < TAPS else bias + row(mb, j)
            high = value.astype(bf16).astype(f32)
            ex[at : at + 1, :] = high
            ex[at + 32 : at + 33, :] = value - high
        wc[j, TAPS * C :, :] = ex[...].astype(bf16)

    def mlp_forward(j):
        def first(ts):
            xhat, scale = norm_parts(xs[ts, :])
            xh_m[j, ts, :] = xhat
            sc[j, ts, 1:2] = scale
            u = (xhat * row(ng, j, 3) + row(ns, j, 3)).astype(bf16).astype(f32)
            acc[0, ts, :] = u * valid[ts, :]

        tiles(first)
        for i in range(n):
            span = slice(i * TOK, (i + 1) * TOK)
            for off, piece in taps_of(acc[0, span, :]):
                u_all[j, span, off * C : (off + 1) * C] = piece.astype(bf16)

        for start in range(0, FF, CHUNK):
            cols = slice(start, start + CHUNK)
            for i in range(n):
                field = nn(u_all[j, i * TOK : (i + 1) * TOK, :], wc[j, :, cols])
                for r0 in range(0, TOK, 16):
                    act, slope = gelu_parts(field[r0 : r0 + 16])
                    part = slice(i * TOK + r0, i * TOK + r0 + 16)
                    a_all[j, part, cols] = act.astype(bf16)
                    g_all[j, part, cols] = slope.astype(bf16)
        for i in range(n):
            span = slice(i * TOK, (i + 1) * TOK)
            branch = nn(a_all[j, span, :], ow[j]) + row(ob, j)
            xs[span, :] = (xs[span, :] + scaled(span, 2 * j + 1) * branch).astype(bf16).astype(f32)

    def mlp_backward(j):
        sb = j * S_BLOCK

        def first(ts):
            grad = (xs[ts, :] * scaled(ts, 2 * j + 1)).astype(bf16)
            db[ts, :] = grad
            return [folded(grad.astype(f32))]

        (small[sb + S_OB : sb + S_OB + 1, :],) = tiles(first)
        db_t[j] = db[...].T
        for start in range(0, FF, CHUNK):
            cols = slice(start, start + CHUNK)
            for i in range(n):
                span = slice(i * TOK, (i + 1) * TOK)
                da = nt(db[span, :], ow[j, cols, :])
                g_all[j, span, cols] = (da * g_all[j, span, cols].astype(f32)).astype(bf16)
        if j == 0:
            move((0, 1))
        acc[...] = jnp.zeros_like(acc)
        for first_off in range(0, TAPS, 2):
            width = min(2, TAPS - first_off)
            for i in range(n):
                at = i * TOK
                moved = nt(
                    g_all[j, at : at + TOK, :], wc[j, first_off * C : (first_off + width) * C, :]
                )
                for s in range(width):
                    off = first_off + s
                    by = (off // 3 - 1) * GRID
                    piece = moved[:, s * C : (s + 1) * C]
                    if by >= 0:
                        acc[off % 3, at + by : at + TOK, :] += piece[: TOK - by]
                    else:
                        acc[off % 3, at : at + TOK + by, :] += piece[-by:]
        for i in range(n):
            span = slice(i * TOK, (i + 1) * TOK)
            left = pltpu.roll(jnp.where(col > 0, acc[0, span, :], 0.0), TOK - 1, 0)
            right = pltpu.roll(jnp.where(col < GRID - 1, acc[2, span, :], 0.0), 1, 0)
            acc[1, span, :] = (acc[1, span, :] + left + right) * valid[span, :]

        def last(ts):
            du = acc[1, ts, :]
            xhat = xh_m[j, ts, :]
            back = norm_back(du, xhat, sc[j, ts, 1:2], row(ng, j, 3))
            xs[ts, :] = (xs[ts, :] + back).astype(bf16).astype(f32)
            return [folded(du * xhat), folded(du)]

        gain, shift = tiles(last)
        small[sb + S_GAIN + 3 : sb + S_GAIN + 4, :] = gain
        small[sb + S_SHIFT + 3 : sb + S_SHIFT + 4, :] = shift

    def mlp_turn(j):
        for off in range(TAPS + 1):
            ut[off * C : (off + 1) * C, :] = u_all[j, :, off * C : (off + 1) * C].T

    def mlp_weights(j, step):
        base, sb = MLP_AT[0] + j * (MLP_AT[1] - MLP_AT[0]), j * S_BLOCK
        cols = slice(step * CHUNK, (step + 1) * CHUNK)
        dow = nn(db_t[j], a_all[j, :, cols])
        gp[packed(base + output_row(step), CHUNK), :] = dow.T.astype(bf16)
        cross = nn(ut[...], g_all[j, :, cols])
        flag_rows = cross[TAPS * C : TAPS * C + 24]
        total = flag_rows[16:17]
        dhb = total
        weight = hw[j, :, cols].astype(f32)
        dweight = jnp.zeros((C, CHUNK), f32)
        b = hb[pl.ds(j, 1), cols]
        for off in range(TAPS):
            piece = cross[off * C : (off + 1) * C]
            factor = mk[off, pl.ds(j, 1), cols]
            flag = flag_rows[off : off + 1]
            dweight = dweight + piece * (factor + (1.0 if off == 4 else 0.0))
            dk = col_sum(piece * weight) + b * flag
            dhb = dhb + factor * flag
            for s in range(CHUNK // C):
                tile = step * (CHUNK // C) + s
                put(sb + S_MK + 16 * tile + off, dk[:, s * C : (s + 1) * C])
        for s in range(CHUNK // C):
            tile = step * (CHUNK // C) + s
            part = slice(s * C, (s + 1) * C)
            put(sb + S_HB + tile, dhb[:, part])
            put(sb + S_MB + tile, total[:, part])
            gp[packed(base + hidden_row(tile), C), :] = dweight[:, part].astype(bf16)

    def attention_backward(j):
        base, sb = ATT_AT[j], j * S_BLOCK

        def first(ts):
            grad = (xs[ts, :] * scaled(ts, 2 * j)).astype(bf16)
            db[ts, :] = grad
            return [folded(grad.astype(f32))]

        (small[sb + S_PB : sb + S_PB + 1, :],) = tiles(first)
        dproj = jnp.zeros((C, C), f32)
        kernel = jnp.concatenate([lk[j, :, 0, :], lk[j, :, 1, :]], axis=1)
        dkernel = [jnp.zeros((1, C), f32) for _ in range(9)]
        dbias = jnp.zeros((1, C), f32)
        for i in range(n):
            span = slice(i * TOK, (i + 1) * TOK)
            dproj = dproj + nn(o_t[j, i], db[span, :])
            do = nt(db[span, :], pw[j]).astype(bf16)
            dprobs = nt(vbd[j, i], do)
            dvals = nn(pt[j, i], do)
            for low, top in SEGS:
                for c0 in range(0, TOK, 128):
                    c1 = min(c0 + 128, TOK)
                    weight = pt[j, i, low:top, c0:c1].astype(f32)
                    dweight = dprobs[low:top, c0:c1]
                    dot = jnp.sum(weight * dweight, axis=0, keepdims=True)
                    pt[j, i, low:top, c0:c1] = (weight * (dweight - dot)).astype(bf16)
            dkeys = nn(pt[j, i], q_a[j, span, :]) * ROOT
            dq = tn(kb[j, i], pt[j, i]) * ROOT
            o_n[span, :] = dq.T.astype(bf16)
            for t in range(2):
                dk = jnp.zeros((CELLS[t], C), f32)
                dv = jnp.zeros((CELLS[t], C), f32)
                for h in (2 * t, 2 * t + 1):
                    dk = dk + jnp.where(head_lanes(h), dkeys[slice(*SEGS[h])], 0.0)
                    dv = dv + jnp.where(head_lanes(h), dvals[slice(*SEGS[h])], 0.0)
                w = wv[j, cell_spans(t)[i], :]
                dw = dv
                for off in range(9):
                    by = near_shift(t, off)
                    part = dv * near[off, place_span[t], :]
                    moved = pltpu.roll(w, (CELLS[t] - by) % CELLS[t], 0) if by else w
                    dkernel[off] = dkernel[off] + col_sum(part * moved)
                    part = part * kernel[off : off + 1]
                    dw = dw + (pltpu.roll(part, by, 0) if by else part)
                dw = dw * kmask[i, place_span[t], :]
                dbias = dbias + col_sum(dw)
                if t == 0:
                    dkeyval = dk + pltpu.roll(dw, 64, 1)
                else:
                    dkeyval = pltpu.roll(dk, 64, 1) + dw
                wv[j, cell_spans(t)[i], :] = dkeyval
        gp[base + R_PROJ : base + R_PROJ + C, :] = dproj.astype(bf16)
        small[sb + S_VB : sb + S_VB + 1, :] = dbias
        for off in range(9):
            small[sb + S_LK + off : sb + S_LK + off + 1, :] = dkernel[off]
        base_perm = 0
        for t, (ref, weight) in enumerate(((p4, p4w), (p2, p2w))):
            span = cells_all(t)
            dkeyval = wv[j, span, :].astype(bf16)
            at = base + R_KV + t * C
            gp[at : at + C, :] = tn(kin[j, span, :], dkeyval).astype(bf16)
            dy = nt(dkeyval, kvw[j, t]) * ge_p[j, span, :]
            xhat = xh_p[j, span, :]
            small[sb + S_GAIN + 1 + t : sb + S_GAIN + 2 + t, :] = col_sum(dy * xhat)
            small[sb + S_SHIFT + 1 + t : sb + S_SHIFT + 2 + t, :] = col_sum(dy)
            dpool = norm_back(dy, xhat, sc_p[j, span, :], row(ng, j, 1 + t)).astype(bf16)
            at = base + (R_P4, R_P2)[t]
            for k in range(STRIDES[t] ** 2):
                gp[at + k * C : at + (k + 1) * C, :] = tn(
                    ref[j, :, k * C : (k + 1) * C], dpool
                ).astype(bf16)
                back = nt(dpool, weight[j, k * C : (k + 1) * C, :]).astype(bf16)
                for i in range(n):
                    pc[base_perm : base_perm + CELLS[t], i * C : (i + 1) * C] = back[
                        i * CELLS[t] : (i + 1) * CELLS[t]
                    ]
                base_perm += CELLS[t]
        at = base + R_Q
        gp[at : at + C, :] = tn(u_a[j], o_n[...]).astype(bf16)
        if j == 1:
            all_here()
            move((0, 0))
        else:
            move((0, 2), (1, 0))
        spread = nn(perm_t[...], pc[...])
        for i in range(n):
            span = slice(i * TOK, (i + 1) * TOK)
            back = nt(o_n[span, :], qw[j])
            acc[0, span, :] = back + spread[:, i * C : (i + 1) * C] * valid[span, :]

        def last(ts):
            du = acc[0, ts, :]
            xhat = xh_a[j, ts, :]
            back = norm_back(du, xhat, sc[j, ts, 0:1], row(ng, j, 0))
            xs[ts, :] = (xs[ts, :] + back).astype(bf16).astype(f32)
            return [folded(o_n[ts, :].astype(f32)), folded(du * xhat), folded(du)]

        bias, gain, shift = tiles(last)
        small[sb + S_QB : sb + S_QB + 1, :] = bias
        small[sb + S_GAIN : sb + S_GAIN + 1, :] = gain
        small[sb + S_SHIFT : sb + S_SHIFT + 1, :] = shift

    def forward(j, carry):
        attention_forward(j)
        mlp_forward(j)
        return carry

    lax.fori_loop(0, BLOCKS, forward, 0)
    out_st[...] = xs[...].astype(bf16)
    leave(out_st, out_ref)
    late.wait()
    xs[...] = cot_ref[...].astype(f32)
    mlp_backward(1)
    attention_backward(1)
    mlp_backward(0)
    attention_backward(0)
    dx_st[...] = xs[...].astype(bf16)
    leave(dx_st, dx_ref)

    def weights(k, carry):
        j = BLOCKS - 1 - k
        mlp_turn(j)
        move_if(k == 0, (1, 1))
        move_if(k == 1, (1, 2), (2, 1), (0, 4))
        mlp_weights(j, 0)
        move_if(k == 0, (0, 3))
        move_if(k == 1, (3, 0))
        mlp_weights(j, 1)
        move_if(k == 0, (2, 0))
        return carry

    lax.fori_loop(0, BLOCKS, weights, 0)
    gp[R_SMALL:, :] = small[...].astype(bf16)
    move((4, 0), (1, 3), (3, 1), (2, 2), (4, 1))
    move((0, 5), (3, 2), (1, 4), (0, 6), (2, 3), (4, 2), (3, 3), (2, 4), (4, 3), (1, 5), (3, 4))
    move((1, 6), (4, 4), (2, 5), (3, 5), (2, 6), (3, 6), (4, 5), (4, 6))
    for piece in pieces:
        piece.drain()
    for made in leaving:
        made.wait()


def compute(own, images, grid_size, keep_mask, x, cot, weights):
    segments, pairs = lax.axis_size("segment"), lax.axis_size("dp") // 2
    inner = min(pairs, 4)
    sizes = (segments, inner, pairs // inner)
    n = images
    rows = n * TOK
    cells = n * sum(CELLS)
    vmem = pl.BlockSpec(memory_space=pltpu.VMEM)
    smem = pl.BlockSpec(memory_space=pltpu.SMEM)
    consts = (jnp.asarray(patch_tokens()), jnp.asarray(cell_places()))
    B = BLOCKS
    scratch = [
        pltpu.VMEM((rows, C), f32),
        pltpu.VMEM((rows, C), f32),
        pltpu.VMEM((TOK, n * C), bf16),
        pltpu.VMEM((B, rows, UW), bf16),
        pltpu.VMEM((UW, rows), bf16),
        pltpu.VMEM((B, UW, FF), bf16),
        pltpu.VMEM((C, FF), f32),
        pltpu.VMEM((B, rows, C), f32),
        pltpu.VMEM((B, rows, C), f32),
        pltpu.VMEM((B, rows, C), f32),
        pltpu.VMEM((B, rows, C), bf16),
        pltpu.VMEM((B, rows, C), bf16),
        pltpu.VMEM((B, n * CELLS[0], 16 * C), bf16),
        pltpu.VMEM((B, n * CELLS[1], 4 * C), bf16),
        pltpu.VMEM((B, cells, C), f32),
        pltpu.VMEM((B, cells, C), f32),
        pltpu.VMEM((B, cells, C), f32),
        pltpu.VMEM((B, cells, C), bf16),
        pltpu.VMEM((B, cells, C), f32),
        pltpu.VMEM((B, n, KEYS, C), bf16),
        pltpu.VMEM((B, n, KEYS, C), bf16),
        pltpu.VMEM((B, n, KEYS, TOK), bf16),
        pltpu.VMEM((B, n, C, TOK), bf16),
        pltpu.VMEM((rows, C), bf16),
        pltpu.VMEM((B, rows, FF), bf16),
        pltpu.VMEM((B, rows, FF), bf16),
        pltpu.VMEM((rows, C), bf16),
        pltpu.VMEM((B, C, rows), bf16),
        pltpu.VMEM((3, rows, C), f32),
        pltpu.VMEM((n, sum(CELLS), C), f32),
        pltpu.VMEM((9, sum(CELLS), C), f32),
        pltpu.VMEM((ROWS - R_SMALL, C), f32),
        pltpu.VMEM((PERM, n * C), bf16),
        pltpu.SMEM((n, 2 * BLOCKS), f32),
        pltpu.VMEM(cot.shape, bf16),
        pltpu.VMEM((PERM, TOK), bf16),
        pltpu.VMEM((TOK, PERM), bf16),
        pltpu.VMEM((rows, C), bf16),
        pltpu.VMEM((rows, C), bf16),
        pltpu.SemaphoreType.DMA((3 + len(PIECES),)),
        pltpu.VMEM((ROWS, C), bf16),
    ] + sum_scratch(sizes)
    anywhere = pl.BlockSpec(memory_space=pl.ANY)
    operands = [vmem] * (2 + len(weights) + len(consts))
    operands[1] = anywhere
    return pl.pallas_call(
        functools.partial(compute_kernel, own, images, sizes),
        out_shape=(
            jax.ShapeDtypeStruct((rows, C), bf16),
            jax.ShapeDtypeStruct((rows, C), bf16),
            jax.ShapeDtypeStruct((ROWS, C), bf16),
        ),
        in_specs=[smem, smem] + operands,
        out_specs=(anywhere,) * 3,
        scratch_shapes=scratch,
        compiler_params=pltpu.CompilerParams(
            collective_id=0, has_side_effects=True, vmem_limit_bytes=63 * 2**20
        ),
        name="compute",
    )(grid_size, keep_mask, x, cot, *weights, *consts)


def unpack_kernel(att, mlp, rest, out_in, dx_in, *refs):
    out_ref, dx_ref = refs[:2]
    gain, shift, qw, qb, p4, p2, kvw, vb, lk, pw, pb, hw, hb, mk, mb, ow, ob = refs[2:]
    out_ref[...] = out_in[...]
    dx_ref[...] = dx_in[...]
    p4[0] = att[R_P4:R_P2, :].astype(f32)
    p2[0] = att[R_P2:R_KV, :].astype(f32)
    for t in range(2):
        kvw[0, t] = att[R_KV + t * C : R_KV + (t + 1) * C, :].astype(f32)
    qw[0] = att[R_Q:R_PROJ, :].astype(f32)
    pw[0] = att[R_PROJ:R_ATT, :].astype(f32)
    for s in range(FF // C):
        hw[0, :, s * C : (s + 1) * C] = mlp[hidden_row(s) : hidden_row(s) + C, :].astype(f32)
    for step in range(FF // CHUNK):
        at = output_row(step)
        ow[0, step * CHUNK : (step + 1) * CHUNK, :] = mlp[at : at + CHUNK, :].astype(f32)

    @pl.when(pl.program_id(0) == BLOCKS - 1)
    def _():
        for j in range(BLOCKS):
            sb = j * S_BLOCK
            head = rest[sb : sb + 48, :].astype(f32)
            gain[j] = head[S_GAIN : S_GAIN + 4]
            shift[j] = head[S_SHIFT : S_SHIFT + 4]
            qb[j : j + 1, :] = head[S_QB : S_QB + 1]
            vb[j, 0:1, :] = head[S_VB : S_VB + 1, 0:64]
            vb[j, 1:2, :] = head[S_VB : S_VB + 1, 64:128]
            pb[j : j + 1, :] = head[S_PB : S_PB + 1]
            ob[j : j + 1, :] = head[S_OB : S_OB + 1]
            lk[j, :, 0, :] = head[S_LK : S_LK + 9, 0:64]
            lk[j, :, 1, :] = head[S_LK : S_LK + 9, 64:128]
            for s in range(FF // C):
                part = slice(s * C, (s + 1) * C)
                hb[j : j + 1, part] = head[S_HB + s : S_HB + s + 1]
                mb[j : j + 1, part] = head[S_MB + s : S_MB + s + 1]
                at = sb + S_MK + 16 * s
                mk[:, j, part] = rest[at : at + 16, :].astype(f32)[0:9]


def unpack(packed, outputs, input_grad, weights):
    streams = (jax.ShapeDtypeStruct(outputs.shape, bf16),) * 2
    by_block = {QW, P4, P2, KVW, PW, HW, OW}
    rest = ROWS - R_SMALL
    stream = pl.BlockSpec((outputs.shape[0] // BLOCKS, C), lambda k: (k, 0))
    specs = []
    for place, w in enumerate(weights):
        if place in by_block:
            zeros = (0,) * (w.ndim - 1)
            specs.append(pl.BlockSpec((1,) + w.shape[1:], lambda k, z=zeros: (BLOCKS - 1 - k,) + z))
        else:
            zeros = (0,) * w.ndim
            specs.append(pl.BlockSpec(w.shape, lambda k, z=zeros: z))
    return pl.pallas_call(
        unpack_kernel,
        out_shape=streams + tuple(jax.ShapeDtypeStruct(w.shape, f32) for w in weights),
        grid=(BLOCKS,),
        in_specs=[
            pl.BlockSpec((R_ATT, C), lambda k: (k, 0)),
            pl.BlockSpec((R_MLP, C), lambda k: (MLP_AT[BLOCKS - 1] // R_MLP + k, 0)),
            pl.BlockSpec((rest, C), lambda k: (R_SMALL // rest, 0)),
            stream,
            stream,
        ],
        out_specs=(stream, stream) + tuple(specs),
        compiler_params=pltpu.CompilerParams(vmem_limit_bytes=63 * 2**20),
        name="unpack",
    )(packed, packed, packed, outputs, input_grad)


def on_device(inputs, grid_size, keep_mask, cotangent, *weights):
    own, per = inputs.shape[:2]
    images = own * per
    flat = (images * TOK, C)
    turned = list(weights)
    turned[LK] = jnp.transpose(turned[LK], (0, 2, 1, 3))
    turned[MK] = jnp.transpose(turned[MK], (1, 0, 2))
    outputs, input_grad, packed = compute(
        own,
        images,
        jnp.transpose(grid_size, (1, 2, 0)),
        jnp.transpose(keep_mask, (1, 2, 0)),
        inputs.reshape(flat),
        cotangent.reshape(flat),
        turned,
    )
    outputs, input_grad, *grads = unpack(packed, outputs, input_grad, turned)
    grads[LK] = jnp.transpose(grads[LK], (0, 2, 1, 3))
    grads[MK] = jnp.transpose(grads[MK], (1, 0, 2))
    return (outputs.reshape(inputs.shape), input_grad.reshape(inputs.shape)) + tuple(grads)


def solution(mesh):
    stream = P("segment", "dp", None, None)
    picked = P(None, "dp", None)
    return jax.shard_map(
        on_device,
        mesh=mesh,
        in_specs=(stream, picked, picked, stream) + (P(),) * 17,
        out_specs=(stream, stream) + (P(),) * 17,
        check_vma=False,
    )
```

profile of v0, /device:TPU:0, one launch (start us, length us, event | category | flops | bytes accessed | tf_op | source)
XLA Modules:
  0.0 89.7 jit_solution(17976246972397748385)
XLA Ops:
  0.7 84.6 %compute.1 = (bf16[1152,128]{1,0:T(8,128)(2,1)}, bf16[1152,128]{1,0:T(8,128)(2,1)}, bf16[10752,128]{1,0:T(8,128)(2,1)}) custom-call(s32[1,2,8]{2,1,0:T(2,128)} %bitcast.19, s32[1,4,8]{2,1,0:T(4,128)} %bitcast.18, bf16[1152,128]{1,0:T(8,128)(2,1)} %bitcast.14, bf16[1152,128]{1,0:T(8,128)(2,1)} %bitcast.15, f32[2,4,128]{2,1,0:T(4,128)} %ng.1, ...), custom_call_target="tpu_custom_call" | custom-call | tf_op jit(solution)/shard_map/compute/pallas_call | solution.py:946
  85.2 4.3 %unpack.1 = (bf16[1152,128]{1,0:T(8,128)(2,1)}, bf16[1152,128]{1,0:T(8,128)(2,1)}, f32[2,4,128]{2,1,0:T(4,128)}, f32[2,4,128]{2,1,0:T(4,128)}, f32[2,128,128]{2,...) custom-call(bf16[10752,128]{1,0:T(8,128)(2,1)} %get-tuple-element.41, ...), custom_call_target="tpu_custom_call" | custom-call | tf_op jit(solution)/shard_map/unpack/pallas_call | solution.py:1015
where the time goes:
time: 89.8 us; the launch traced here: 89.7 us
  Pallas kernels  88.8 us (99%)
    pallas_call x1, Pallas kernels, compute(): pl.pallas_call(functools.partial(compute_kernel, own, images, sizes), out...  84.6 us
    pallas_call x1, Pallas kernels, unpack(): pl.pallas_call(unpack_kernel, out_shape=streams + tuple((jax.ShapeDtypeSt...  4.26 us

commit v1 on v0

--- a/solution.py
+++ b/solution.py
@@ -321,18 +321,18 @@
     ns,
     qw,
     qb,
-    p4w,
-    p2w,
+    p4w_in,
+    p2w_in,
     kvw,
     vb,
     lk,
     pw,
     pb,
-    hw,
+    hw_in,
     hb,
     mk,
     mb,
-    ow,
+    ow_in,
     ob,
     tokens,
     places,
@@ -374,6 +374,10 @@
     pc,
     scale_ref,
     cot_ref,
+    hw,
+    p4w,
+    p2w,
+    ow,
     perm,
     perm_t,
     out_st,
@@ -393,12 +397,18 @@
     rows = n * TOK
     seg, dp = lax.axis_index("segment"), lax.axis_index("dp")
     all_here = greet(seg, dp, *sizes)
-    late = pltpu.make_async_copy(cot_in, cot_ref, sems.at[0])
-    late.start()
+    late = [
+        pltpu.make_async_copy(src, dst, sems.at[k])
+        for k, (src, dst) in enumerate(
+            ((hw_in, hw), (p4w_in, p4w), (p2w_in, p2w), (ow_in, ow), (cot_in, cot_ref))
+        )
+    ]
+    for made in late:
+        made.start()
     leaving = []
 
     def leave(src, dst):
-        made = pltpu.make_async_copy(src, dst, sems.at[1 + len(leaving)])
+        made = pltpu.make_async_copy(src, dst, sems.at[len(late) + len(leaving)])
         made.start()
         leaving.append(made)
 
@@ -638,21 +648,21 @@
             xh_m[j, ts, :] = xhat
             sc[j, ts, 1:2] = scale
             u = (xhat * row(ng, j, 3) + row(ns, j, 3)).astype(bf16).astype(f32)
-            acc[0, ts, :] = u * valid[ts, :]
+            acc[ts, :] = u * valid[ts, :]
 
         tiles(first)
         for i in range(n):
             span = slice(i * TOK, (i + 1) * TOK)
-            for off, piece in taps_of(acc[0, span, :]):
+            for off, piece in taps_of(acc[span, :]):
                 u_all[j, span, off * C : (off + 1) * C] = piece.astype(bf16)
 
-        for start in range(0, FF, CHUNK):
-            cols = slice(start, start + CHUNK)
-            for i in range(n):
-                field = nn(u_all[j, i * TOK : (i + 1) * TOK, :], wc[j, :, cols])
-                for r0 in range(0, TOK, 16):
-                    act, slope = gelu_parts(field[r0 : r0 + 16])
-                    part = slice(i * TOK + r0, i * TOK + r0 + 16)
+        for i in range(n):
+            field = nn(u_all[j, i * TOK : (i + 1) * TOK, :], wc[j])
+            for r0 in range(0, TOK, 16):
+                part = slice(i * TOK + r0, i * TOK + r0 + 16)
+                for start in range(0, FF, CHUNK):
+                    cols = slice(start, start + CHUNK)
+                    act, slope = gelu_parts(field[r0 : r0 + 16, cols])
                     a_all[j, part, cols] = act.astype(bf16)
                     g_all[j, part, cols] = slope.astype(bf16)
         for i in range(n):
@@ -670,38 +680,29 @@
 
         (small[sb + S_OB : sb + S_OB + 1, :],) = tiles(first)
         db_t[j] = db[...].T
-        for start in range(0, FF, CHUNK):
-            cols = slice(start, start + CHUNK)
-            for i in range(n):
-                span = slice(i * TOK, (i + 1) * TOK)
-                da = nt(db[span, :], ow[j, cols, :])
-                g_all[j, span, cols] = (da * g_all[j, span, cols].astype(f32)).astype(bf16)
+        for i in range(n):
+            span = slice(i * TOK, (i + 1) * TOK)
+            da = nt(db[span, :], ow[j])
+            g_all[j, span, :] = (da * g_all[j, span, :].astype(f32)).astype(bf16)
         if j == 0:
             move((0, 1))
-        acc[...] = jnp.zeros_like(acc)
-        for first_off in range(0, TAPS, 2):
-            width = min(2, TAPS - first_off)
-            for i in range(n):
-                at = i * TOK
-                moved = nt(
-                    g_all[j, at : at + TOK, :], wc[j, first_off * C : (first_off + width) * C, :]
-                )
-                for s in range(width):
-                    off = first_off + s
-                    by = (off // 3 - 1) * GRID
-                    piece = moved[:, s * C : (s + 1) * C]
-                    if by >= 0:
-                        acc[off % 3, at + by : at + TOK, :] += piece[: TOK - by]
-                    else:
-                        acc[off % 3, at : at + TOK + by, :] += piece[-by:]
         for i in range(n):
             span = slice(i * TOK, (i + 1) * TOK)
-            left = pltpu.roll(jnp.where(col > 0, acc[0, span, :], 0.0), TOK - 1, 0)
-            right = pltpu.roll(jnp.where(col < GRID - 1, acc[2, span, :], 0.0), 1, 0)
-            acc[1, span, :] = (acc[1, span, :] + left + right) * valid[span, :]
+            moved = nt(g_all[j, span, :], wc[j, : TAPS * C, :])
+            sides = []
+            for col_off in range(3):
+                total = None
+                for row_off in range(3):
+                    off = row_off * 3 + col_off
+                    piece = shifted_rows(moved[:, off * C : (off + 1) * C], (1 - row_off) * GRID)
+                    total = piece if total is None else total + piece
+                sides.append(total)
+            left = pltpu.roll(jnp.where(col > 0, sides[0], 0.0), TOK - 1, 0)
+            right = pltpu.roll(jnp.where(col < GRID - 1, sides[2], 0.0), 1, 0)
+            acc[span, :] = (sides[1] + left + right) * valid[span, :]
 
         def last(ts):
-            du = acc[1, ts, :]
+            du = acc[ts, :]
             xhat = xh_m[j, ts, :]
             back = norm_back(du, xhat, sc[j, ts, 1:2], row(ng, j, 3))
             xs[ts, :] = (xs[ts, :] + back).astype(bf16).astype(f32)
@@ -832,10 +833,10 @@
         for i in range(n):
             span = slice(i * TOK, (i + 1) * TOK)
             back = nt(o_n[span, :], qw[j])
-            acc[0, span, :] = back + spread[:, i * C : (i + 1) * C] * valid[span, :]
+            acc[span, :] = back + spread[:, i * C : (i + 1) * C] * valid[span, :]
 
         def last(ts):
-            du = acc[0, ts, :]
+            du = acc[ts, :]
             xhat = xh_a[j, ts, :]
             back = norm_back(du, xhat, sc[j, ts, 0:1], row(ng, j, 0))
             xs[ts, :] = (xs[ts, :] + back).astype(bf16).astype(f32)
@@ -851,10 +852,11 @@
         mlp_forward(j)
         return carry
 
+    for made in late:
+        made.wait()
     lax.fori_loop(0, BLOCKS, forward, 0)
     out_st[...] = xs[...].astype(bf16)
     leave(out_st, out_ref)
-    late.wait()
     xs[...] = cot_ref[...].astype(f32)
     mlp_backward(1)
     attention_backward(1)
@@ -926,23 +928,28 @@
         pltpu.VMEM((B, rows, FF), bf16),
         pltpu.VMEM((rows, C), bf16),
         pltpu.VMEM((B, C, rows), bf16),
-        pltpu.VMEM((3, rows, C), f32),
+        pltpu.VMEM((rows, C), f32),
         pltpu.VMEM((n, sum(CELLS), C), f32),
         pltpu.VMEM((9, sum(CELLS), C), f32),
         pltpu.VMEM((ROWS - R_SMALL, C), f32),
         pltpu.VMEM((PERM, n * C), bf16),
         pltpu.SMEM((n, 2 * BLOCKS), f32),
         pltpu.VMEM(cot.shape, bf16),
+        pltpu.VMEM(weights[HW].shape, bf16),
+        pltpu.VMEM(weights[P4].shape, bf16),
+        pltpu.VMEM(weights[P2].shape, bf16),
+        pltpu.VMEM(weights[OW].shape, bf16),
         pltpu.VMEM((PERM, TOK), bf16),
         pltpu.VMEM((TOK, PERM), bf16),
         pltpu.VMEM((rows, C), bf16),
         pltpu.VMEM((rows, C), bf16),
-        pltpu.SemaphoreType.DMA((3 + len(PIECES),)),
+        pltpu.SemaphoreType.DMA((7 + len(PIECES),)),
         pltpu.VMEM((ROWS, C), bf16),
     ] + sum_scratch(sizes)
     anywhere = pl.BlockSpec(memory_space=pl.ANY)
     operands = [vmem] * (2 + len(weights) + len(consts))
-    operands[1] = anywhere
+    for place in (1, 2 + HW, 2 + P4, 2 + P2, 2 + OW):
+        operands[place] = anywhere
     return pl.pallas_call(
         functools.partial(compute_kernel, own, images, sizes),
         out_shape=(

time: 89.8 us -> 88.3 us (0.983)
  Pallas kernels: 88.8 us -> 87.3 us
    pallas_call x1, Pallas kernels: 84.6 us -> 83 us  [compute(): pl.pallas_call(functools.partial(compute_kernel, own, images, sizes), out...]
where the time goes in v1:
time: 88.3 us; the launch traced here: 88.1 us
  Pallas kernels  87.3 us (99%)
    pallas_call x1, Pallas kernels, compute(): pl.pallas_call(functools.partial(compute_kernel, own, images, sizes), out...  83 us
    pallas_call x1, Pallas kernels, unpack(): pl.pallas_call(unpack_kernel, out_shape=streams + tuple((jax.ShapeDtypeSt...  4.26 us

profile of v1, /device:TPU:0, one launch (start us, length us, event | category | flops | bytes accessed | tf_op | source)
XLA Modules:
  0.0 88.1 jit_solution(18257377564700689482)
XLA Ops:
  0.7 83.0 %compute.1 = (bf16[1152,128]{1,0:T(8,128)(2,1)}, bf16[1152,128]{1,0:T(8,128)(2,1)}, bf16[10752,128]{1,0:T(8,128)(2,1)}) custom-call(s32[1,2,8]{2,1,0:T(2,128)} %bitcast.19, s32[1,4,8]{2,1,0:T(4,128)} %bitcast.18, bf16[1152,128]{1,0:T(8,128)(2,1)} %bitcast.14, bf16[1152,128]{1,0:T(8,128)(2,1)} %bitcast.15, f32[2,4,128]{2,1,0:T(4,128)} %ng.1, ...), custom_call_target="tpu_custom_call" | custom-call | tf_op jit(solution)/shard_map/compute/pallas_call | solution.py:953
  83.7 4.3 %unpack.1 = (bf16[1152,128]{1,0:T(8,128)(2,1)}, bf16[1152,128]{1,0:T(8,128)(2,1)}, f32[2,4,128]{2,1,0:T(4,128)}, f32[2,4,128]{2,1,0:T(4,128)}, f32[2,128,128]{2,...) custom-call(bf16[10752,128]{1,0:T(8,128)(2,1)} %get-tuple-element.41, ...), custom_call_target="tpu_custom_call" | custom-call | tf_op jit(solution)/shard_map/unpack/pallas_call | solution.py:1022

commit v2 on v1

--- a/solution.py
+++ b/solution.py
@@ -16,10 +16,14 @@
 BLOCKS = 2
 SIDES = (6, 12)
 STRIDES = (4, 2)
+WIDTHS = (8, 12)
 CELLS = (48, 144)
 SEGS = ((0, 48), (48, 96), (96, 240), (240, 384))
 KEYS = 384
-PERM = 16 * 48 + 4 * 144
+GROUP = 4 * GRID
+GROUPS = TOK // GROUP
+PATCH = (8, 24)
+PATCHES = 16 * PATCH[0] + 4 * PATCH[1]
 TAPS = 9
 UW = TAPS * C + C
 CHUNK = 512
@@ -69,28 +73,28 @@
     return step * 2 * CHUNK + CHUNK
 
 
-def patch_tokens():
-    tokens = np.full((8, PERM), -1.0, np.float32)
+def patch_matrix():
+    matrix = np.zeros((PATCHES, GROUP), np.float32)
     base = 0
-    for stride, side, cells in zip(STRIDES, SIDES, CELLS):
+    for stride, side, width, count in zip(STRIDES, SIDES, WIDTHS, PATCH):
         for row_off in range(stride):
             for col_off in range(stride):
-                for a in range(side):
+                for a in range(4 // stride):
                     for b in range(side):
                         token = (a * stride + row_off) * GRID + b * stride + col_off
-                        tokens[:, base + a * side + b] = token
-                base += cells
-    return tokens
+                        matrix[base + a * width + b, token] = 1.0
+                base += count
+    return matrix
 
 
 def cell_places():
     places = np.full((2, sum(CELLS), 128), 99.0, np.float32)
     base = 0
-    for side, cells in zip(SIDES, CELLS):
+    for side, width, cells in zip(SIDES, WIDTHS, CELLS):
         for a in range(side):
             for b in range(side):
-                places[0, base + a * side + b] = a
-                places[1, base + a * side + b] = b
+                places[0, base + a * width + b] = a
+                places[1, base + a * width + b] = b
         base += cells
     return places
 
@@ -266,7 +270,7 @@
             self.add(into, mine, received, self.share)
 
     def add(self, dst, first, others, count):
-        step = next(size for size in (128, 96, 80, 64, 48, 32, 16) if count % size == 0)
+        step = next(size for size in (512, 384, 256, 192, 128, 96, 64, 48, 32, 16) if count % size == 0)
 
         def body(t, carry):
             at = t * step
@@ -334,7 +338,8 @@
     mb,
     ow_in,
     ob,
-    tokens,
+    to_patches,
+    from_patches,
     places,
     out_ref,
     dx_ref,
@@ -371,15 +376,12 @@
     kmask,
     near,
     small,
-    pc,
     scale_ref,
     cot_ref,
     hw,
     p4w,
     p2w,
     ow,
-    perm,
-    perm_t,
     out_st,
     dx_st,
     sems,
@@ -519,24 +521,6 @@
             near[off, span, :] = jnp.where(ok, 1.0, 0.0)
         base += CELLS[t]
 
-    base = start = 0
-    for t in range(2):
-        span, stride = slice(start, start + CELLS[t]), STRIDES[t]
-        corner = places[0, span, :] * float(stride * GRID) + places[1, span, :] * float(stride)
-        for k in range(stride * stride):
-            token = corner + float(k // stride * GRID + k % stride)
-            for c0 in range(0, TOK, 128):
-                width = min(128, TOK - c0)
-                here = lax.broadcasted_iota(jnp.int32, (CELLS[t], width), 1).astype(f32) + float(c0)
-                block = jnp.where(token[:, :width] == here, 1.0, 0.0)
-                perm[base : base + CELLS[t], c0 : c0 + width] = block.astype(bf16)
-            base += CELLS[t]
-        start += CELLS[t]
-    for r0 in range(0, TOK, TILE):
-        here = lax.broadcasted_iota(jnp.int32, (TILE, PERM), 0).astype(f32) + float(r0)
-        block = jnp.where(tokens[0:1, :] == here, 1.0, 0.0)
-        perm_t[r0 : r0 + TILE, :] = block.astype(bf16)
-
     xs[...] = x_ref[...].astype(f32)
 
     def scaled(span, k):
@@ -554,7 +538,7 @@
     own_half = (half, jnp.logical_not(half))
 
     def near_shift(t, off):
-        return ((off // 3 - 1) * SIDES[t] + off % 3 - 1) % CELLS[t]
+        return ((off // 3 - 1) * WIDTHS[t] + off % 3 - 1) % CELLS[t]
 
     def attention_forward(j):
         build_wc(j)
@@ -571,15 +555,17 @@
             u = u_a[j, span, :]
             q_a[j, span, :] = (nn(u, qw[j]) + row(qb, j)).astype(bf16)
             um[:, i * C : (i + 1) * C] = (u.astype(f32) * valid[span, :]).astype(bf16)
-        pc[...] = nn(perm[...], um[...]).astype(bf16)
+        groups = [
+            nn(to_patches[...], um[g * GROUP : (g + 1) * GROUP, :]) for g in range(GROUPS)
+        ]
         base = 0
         for t, ref in enumerate((p4, p2)):
             for k in range(STRIDES[t] ** 2):
                 for i in range(n):
-                    ref[j, i * CELLS[t] : (i + 1) * CELLS[t], k * C : (k + 1) * C] = pc[
-                        base : base + CELLS[t], i * C : (i + 1) * C
-                    ]
-                base += CELLS[t]
+                    pieces = [x[base : base + PATCH[t], i * C : (i + 1) * C] for x in groups]
+                    part = slice(i * CELLS[t], (i + 1) * CELLS[t])
+                    ref[j, part, k * C : (k + 1) * C] = jnp.concatenate(pieces, axis=0).astype(bf16)
+                base += PATCH[t]
         for t, (ref, weight) in enumerate(((p4, p4w), (p2, p2w))):
             xhat, scale = norm_parts(nn(ref[j], weight[j]))
             act, slope = gelu_parts(xhat * row(ng, j, 1 + t) + row(ns, j, 1 + t))
@@ -800,7 +786,7 @@
         small[sb + S_VB : sb + S_VB + 1, :] = dbias
         for off in range(9):
             small[sb + S_LK + off : sb + S_LK + off + 1, :] = dkernel[off]
-        base_perm = 0
+        backs = []
         for t, (ref, weight) in enumerate(((p4, p4w), (p2, p2w))):
             span = cells_all(t)
             dkeyval = wv[j, span, :].astype(bf16)
@@ -816,12 +802,7 @@
                 gp[at + k * C : at + (k + 1) * C, :] = tn(
                     ref[j, :, k * C : (k + 1) * C], dpool
                 ).astype(bf16)
-                back = nt(dpool, weight[j, k * C : (k + 1) * C, :]).astype(bf16)
-                for i in range(n):
-                    pc[base_perm : base_perm + CELLS[t], i * C : (i + 1) * C] = back[
-                        i * CELLS[t] : (i + 1) * CELLS[t]
-                    ]
-                base_perm += CELLS[t]
+                backs.append((t, nt(dpool, weight[j, k * C : (k + 1) * C, :])))
         at = base + R_Q
         gp[at : at + C, :] = tn(u_a[j], o_n[...]).astype(bf16)
         if j == 1:
@@ -829,11 +810,21 @@
             move((0, 0))
         else:
             move((0, 2), (1, 0))
-        spread = nn(perm_t[...], pc[...])
         for i in range(n):
             span = slice(i * TOK, (i + 1) * TOK)
-            back = nt(o_n[span, :], qw[j])
-            acc[span, :] = back + spread[:, i * C : (i + 1) * C] * valid[span, :]
+            acc[span, :] = nt(o_n[span, :], qw[j])
+        for g in range(GROUPS):
+            images_of = []
+            for i in range(n):
+                pieces = [
+                    back[i * CELLS[t] + g * PATCH[t] : i * CELLS[t] + (g + 1) * PATCH[t]]
+                    for t, back in backs
+                ]
+                images_of.append(jnp.concatenate(pieces, axis=0).astype(bf16))
+            spread = nn(from_patches[...], jnp.concatenate(images_of, axis=1))
+            for i in range(n):
+                span = slice(i * TOK + g * GROUP, i * TOK + (g + 1) * GROUP)
+                acc[span, :] += spread[:, i * C : (i + 1) * C] * valid[span, :]
 
         def last(ts):
             du = acc[ts, :]
@@ -860,6 +851,7 @@
     xs[...] = cot_ref[...].astype(f32)
     mlp_backward(1)
     attention_backward(1)
+    mlp_turn(1)
     mlp_backward(0)
     attention_backward(0)
     dx_st[...] = xs[...].astype(bf16)
@@ -867,7 +859,7 @@
 
     def weights(k, carry):
         j = BLOCKS - 1 - k
-        mlp_turn(j)
+        pl.when(k == 1)(lambda: mlp_turn(0))
         move_if(k == 0, (1, 1))
         move_if(k == 1, (1, 2), (2, 1), (0, 4))
         mlp_weights(j, 0)
@@ -897,7 +889,12 @@
     cells = n * sum(CELLS)
     vmem = pl.BlockSpec(memory_space=pltpu.VMEM)
     smem = pl.BlockSpec(memory_space=pltpu.SMEM)
-    consts = (jnp.asarray(patch_tokens()), jnp.asarray(cell_places()))
+    matrix = patch_matrix()
+    consts = (
+        jnp.asarray(matrix, bf16),
+        jnp.asarray(matrix.T, bf16),
+        jnp.asarray(cell_places()),
+    )
     B = BLOCKS
     scratch = [
         pltpu.VMEM((rows, C), f32),
@@ -932,15 +929,12 @@
         pltpu.VMEM((n, sum(CELLS), C), f32),
         pltpu.VMEM((9, sum(CELLS), C), f32),
         pltpu.VMEM((ROWS - R_SMALL, C), f32),
-        pltpu.VMEM((PERM, n * C), bf16),
         pltpu.SMEM((n, 2 * BLOCKS), f32),
         pltpu.VMEM(cot.shape, bf16),
         pltpu.VMEM(weights[HW].shape, bf16),
         pltpu.VMEM(weights[P4].shape, bf16),
         pltpu.VMEM(weights[P2].shape, bf16),
         pltpu.VMEM(weights[OW].shape, bf16),
-        pltpu.VMEM((PERM, TOK), bf16),
-        pltpu.VMEM((TOK, PERM), bf16),
         pltpu.VMEM((rows, C), bf16),
         pltpu.VMEM((rows, C), bf16),
         pltpu.SemaphoreType.DMA((7 + len(PIECES),)),

time: 88.3 us -> 85.4 us (0.967)
  Pallas kernels: 87.3 us -> 83.8 us
    pallas_call x1, Pallas kernels: 83 us -> 79.5 us  [compute(): pl.pallas_call(functools.partial(compute_kernel, own, images, sizes), out...]
where the time goes in v2:
time: 85.4 us; the launch traced here: 84.6 us
  Pallas kernels  83.8 us (98%)
    pallas_call x1, Pallas kernels, compute(): pl.pallas_call(functools.partial(compute_kernel, own, images, sizes), out...  79.5 us
    pallas_call x1, Pallas kernels, unpack(): pl.pallas_call(unpack_kernel, out_shape=streams + tuple((jax.ShapeDtypeSt...  4.26 us

profile of v2, /device:TPU:0, one launch (start us, length us, event | category | flops | bytes accessed | tf_op | source)
XLA Modules:
  0.0 84.6 jit_solution(269680415375562484)
XLA Ops:
  0.7 79.5 %compute.1 = (bf16[1152,128]{1,0:T(8,128)(2,1)}, bf16[1152,128]{1,0:T(8,128)(2,1)}, bf16[10752,128]{1,0:T(8,128)(2,1)}) custom-call(s32[1,2,8]{2,1,0:T(2,128)} %bitcast.19, s32[1,4,8]{2,1,0:T(4,128)} %bitcast.18, bf16[1152,128]{1,0:T(8,128)(2,1)} %bitcast.14, bf16[1152,128]{1,0:T(8,128)(2,1)} %bitcast.15, f32[2,4,128]{2,1,0:T(4,128)} %ng.1, ...), custom_call_target="tpu_custom_call" | custom-call | tf_op jit(solution)/shard_map/compute/pallas_call | solution.py:947
  80.2 4.3 %unpack.1 = (bf16[1152,128]{1,0:T(8,128)(2,1)}, bf16[1152,128]{1,0:T(8,128)(2,1)}, f32[2,4,128]{2,1,0:T(4,128)}, f32[2,4,128]{2,1,0:T(4,128)}, f32[2,128,128]{2,...) custom-call(bf16[10752,128]{1,0:T(8,128)(2,1)} %get-tuple-element.41, ...), custom_call_target="tpu_custom_call" | custom-call | tf_op jit(solution)/shard_map/unpack/pallas_call | solution.py:1016

commit v3 on v2

--- a/solution.py
+++ b/solution.py
@@ -436,9 +436,6 @@
                 rows_of = pl.ds(PIECES[p][0], PIECES[p][1])
                 leave(total_ref.at[rows_of, :], summed_ref.at[rows_of, :])
 
-    def move_if(now, *steps):
-        pl.when(now)(lambda: move(*steps))
-
     lane = lax.broadcasted_iota(jnp.int32, (8, 128), 1)[0:1]
 
     def head_lanes(h):
@@ -459,7 +456,7 @@
         small[pl.ds(at, 1), :] = value
 
     def packed(start, count):
-        return pl.ds(pl.multiple_of(start, 128), count)
+        return pl.ds(start, count)
 
     def shifted_rows(v, by):
         if by == 0:
@@ -687,6 +684,9 @@
             right = pltpu.roll(jnp.where(col < GRID - 1, sides[2], 0.0), 1, 0)
             acc[span, :] = (sides[1] + left + right) * valid[span, :]
 
+        if j == 0:
+            mlp_weights(1, 0)
+
         def last(ts):
             du = acc[ts, :]
             xhat = xh_m[j, ts, :]
@@ -700,14 +700,14 @@
 
     def mlp_turn(j):
         for off in range(TAPS + 1):
-            ut[off * C : (off + 1) * C, :] = u_all[j, :, off * C : (off + 1) * C].T
+            ut[j, off * C : (off + 1) * C, :] = u_all[j, :, off * C : (off + 1) * C].T
 
     def mlp_weights(j, step):
         base, sb = MLP_AT[0] + j * (MLP_AT[1] - MLP_AT[0]), j * S_BLOCK
         cols = slice(step * CHUNK, (step + 1) * CHUNK)
         dow = nn(db_t[j], a_all[j, :, cols])
         gp[packed(base + output_row(step), CHUNK), :] = dow.T.astype(bf16)
-        cross = nn(ut[...], g_all[j, :, cols])
+        cross = nn(ut[j], g_all[j, :, cols])
         flag_rows = cross[TAPS * C : TAPS * C + 24]
         total = flag_rows[16:17]
         dhb = total
@@ -782,6 +782,8 @@
                 else:
                     dkeyval = pltpu.roll(dk, 64, 1) + dw
                 wv[j, cell_spans(t)[i], :] = dkeyval
+            if j == 0 and i == 0:
+                mlp_weights(1, 1)
         gp[base + R_PROJ : base + R_PROJ + C, :] = dproj.astype(bf16)
         small[sb + S_VB : sb + S_VB + 1, :] = dbias
         for off in range(9):
@@ -809,7 +811,7 @@
             all_here()
             move((0, 0))
         else:
-            move((0, 2), (1, 0))
+            move((1, 0), (2, 0), (0, 2))
         for i in range(n):
             span = slice(i * TOK, (i + 1) * TOK)
             acc[span, :] = nt(o_n[span, :], qw[j])
@@ -853,27 +855,18 @@
     attention_backward(1)
     mlp_turn(1)
     mlp_backward(0)
+    mlp_turn(0)
     attention_backward(0)
     dx_st[...] = xs[...].astype(bf16)
     leave(dx_st, dx_ref)
-
-    def weights(k, carry):
-        j = BLOCKS - 1 - k
-        pl.when(k == 1)(lambda: mlp_turn(0))
-        move_if(k == 0, (1, 1))
-        move_if(k == 1, (1, 2), (2, 1), (0, 4))
-        mlp_weights(j, 0)
-        move_if(k == 0, (0, 3))
-        move_if(k == 1, (3, 0))
-        mlp_weights(j, 1)
-        move_if(k == 0, (2, 0))
-        return carry
-
-    lax.fori_loop(0, BLOCKS, weights, 0)
+    move((1, 1), (2, 1))
+    mlp_weights(0, 0)
+    move((3, 0), (0, 3))
+    mlp_weights(0, 1)
     gp[R_SMALL:, :] = small[...].astype(bf16)
-    move((4, 0), (1, 3), (3, 1), (2, 2), (4, 1))
-    move((0, 5), (3, 2), (1, 4), (0, 6), (2, 3), (4, 2), (3, 3), (2, 4), (4, 3), (1, 5), (3, 4))
-    move((1, 6), (4, 4), (2, 5), (3, 5), (2, 6), (3, 6), (4, 5), (4, 6))
+    move((4, 0), (3, 1), (1, 2), (4, 1), (0, 4), (2, 2), (3, 2), (1, 3), (4, 2), (2, 3), (3, 3))
+    move((0, 5), (1, 4), (4, 3), (0, 6), (2, 4), (3, 4), (4, 4), (1, 5), (1, 6), (2, 5), (3, 5))
+    move((2, 6), (3, 6), (4, 5), (4, 6))
     for piece in pieces:
         piece.drain()
     for made in leaving:
@@ -901,7 +894,7 @@
         pltpu.VMEM((rows, C), f32),
         pltpu.VMEM((TOK, n * C), bf16),
         pltpu.VMEM((B, rows, UW), bf16),
-        pltpu.VMEM((UW, rows), bf16),
+        pltpu.VMEM((B, UW, rows), bf16),
         pltpu.VMEM((B, UW, FF), bf16),
         pltpu.VMEM((C, FF), f32),
         pltpu.VMEM((B, rows, C), f32),

time: 85.4 us -> 86.1 us (level)
  Pallas kernels: 83.8 us -> 85.1 us
    pallas_call x1, Pallas kernels: 79.5 us -> 80.8 us  [compute(): pl.pallas_call(functools.partial(compute_kernel, own, images, sizes), out...]
where the time goes in v3:
time: 86.1 us; the launch traced here: 85.9 us
  Pallas kernels  85.1 us (99%)
  between operations  0.87 us (1%)
    pallas_call x1, Pallas kernels, compute(): pl.pallas_call(functools.partial(compute_kernel, own, images, sizes), out...  80.8 us
    pallas_call x1, Pallas kernels, unpack(): pl.pallas_call(unpack_kernel, out_shape=streams + tuple((jax.ShapeDtypeSt...  4.26 us

profile of v3, /device:TPU:0, one launch (start us, length us, event | category | flops | bytes accessed | tf_op | source)
XLA Modules:
  0.0 85.9 jit_solution(16236004731588267751)
XLA Ops:
  0.7 80.8 %compute.1 = (bf16[1152,128]{1,0:T(8,128)(2,1)}, bf16[1152,128]{1,0:T(8,128)(2,1)}, bf16[10752,128]{1,0:T(8,128)(2,1)}) custom-call(s32[1,2,8]{2,1,0:T(2,128)} %bitcast.19, s32[1,4,8]{2,1,0:T(4,128)} %bitcast.18, bf16[1152,128]{1,0:T(8,128)(2,1)} %bitcast.14, bf16[1152,128]{1,0:T(8,128)(2,1)} %bitcast.15, f32[2,4,128]{2,1,0:T(4,128)} %ng.1, ...), custom_call_target="tpu_custom_call" | custom-call | tf_op jit(solution)/shard_map/compute/pallas_call | solution.py:940
  81.5 4.3 %unpack.1 = (bf16[1152,128]{1,0:T(8,128)(2,1)}, bf16[1152,128]{1,0:T(8,128)(2,1)}, f32[2,4,128]{2,1,0:T(4,128)}, f32[2,4,128]{2,1,0:T(4,128)}, f32[2,128,128]{2,...) custom-call(bf16[10752,128]{1,0:T(8,128)(2,1)} %get-tuple-element.41, ...), custom_call_target="tpu_custom_call" | custom-call | tf_op jit(solution)/shard_map/unpack/pallas_call | solution.py:1009
